TPU v7x, 32 devices: a whole 2x2x4 slice. The times are simulated.
32 devices in a mesh: gx: 4 (over z), yz: 8 (over y, x, core).
Axes of the slice: x: 2, y: 2, z: 4, core: 2. Of those that a mesh axis runs over, the one named last changes fastest.
Arguments:
- features: bfloat16 [384, 96, 512], P(('gx', 'yz')), may hold values from -6 to 6
- occupancy: int32 [384, 512], P(('gx', 'yz')), may hold values 0 or 1
- neighbours: int32 [384, 27], P(('gx', 'yz')), may hold values from 0 to 84, as said below
- exports: int32 [256], P(('gx', 'yz')), may hold values from 0 to 11, as said below
- coarse_map: int32 [384, 2], P(('gx', 'yz')), may hold values from 0 to 7, as said below
- owners: int32 [128], P(('gx', 'yz')), may hold values from 0 to 7, as said below
- w_sub: bfloat16 [27, 96, 96], replicated, may hold values from -0.15625 to 0.15625
- w_down: bfloat16 [8, 192, 96], replicated, may hold values from -0.3125 to 0.3125
- cotangent: bfloat16 [256, 192, 512], P(('gx', 'yz')), may hold values from -6 to 6
Outputs:
- coarse: bfloat16 [256, 192, 512], P(('gx', 'yz'))
- grad_features: bfloat16 [384, 96, 512], P(('gx', 'yz'))
- grad_sub: float32 [27, 96, 96], replicated
- grad_down: float32 [8, 192, 96], replicated
Inputs may be any that keep to these rules, and one draw needn't show every extreme that they name: `neighbours`: entry 13 of a brick is its own slot. Entries follow the geometry of a map of 8-voxel bricks in which device (i, j) holds a region of 4 x 4 x 2 brick cells beside the regions of (i +- 1, j +- 1); a brick met at offset k meets the first at the opposite offset. Entries that point to another device name only bricks on that device's side faces. `exports`: each device's 8 entries are distinct slots of its bricks that lie on its region's side faces, and every such brick is listed. `coarse_map`: column 0 is the coarse cell (0 to 3), column 1 the octant; every coarse cell of every device holds exactly 3 of its fine bricks, in distinct octants. The 4 coarse cells of one device have distinct owners; in every gx slab one owner is named by every device of the slab.
All inputs are finite; a program needn't handle non-finite values. No bound on the sum of `occupancy` on one device may be relied on, other than what follows from the above.
Results may differ from a plain program's by a relative error of at most 0.0062.
Values may be sent and summed in bfloat16 or wider, within the bound.
A program may use at most 320 MiB of HBM per device.

v0:
```python
import jax
import jax.numpy as jnp
from jax import lax
from jax.sharding import PartitionSpec as P

EDGE = 8


def padded_2(x, sides, width):
    for axis, dim in sides:
        size, length = (lax.axis_size(axis), x.shape[dim])
        up = [(i, (i + 1) % size) for i in range(size - 1)]
        down = [(j, i) for i, j in up]
        last = lax.slice_in_dim(x, length - width, length, axis=dim)
        initial = lax.slice_in_dim(x, 0, width, axis=dim)
        before = lax.ppermute(last, axis, up)
        after = lax.ppermute(initial, axis, down)
        x = jnp.concatenate([before, x, after], axis=dim)
    return x


def silu_slope(values):
    sig = jax.nn.sigmoid(values)
    return sig * (1.0 + values * (1.0 - sig))


def layer_span(shift, cube_edge):
    if shift < 0:
        return (slice(cube_edge - 1, cube_edge), slice(0, 1))
    if shift > 0:
        return (slice(0, 1), slice(cube_edge + 1, cube_edge + 2))
    return (slice(0, cube_edge), slice(1, cube_edge + 1))


def pad_bricks(lookup, neighbour_ids, cube_edge):
    channels = lookup.shape[1]
    blocks = lookup.reshape(lookup.shape[0], channels, cube_edge, cube_edge, cube_edge)
    padded = jnp.zeros(
        (neighbour_ids.shape[0], channels, cube_edge + 2, cube_edge + 2, cube_edge + 2),
        lookup.dtype,
    )
    for offset in range(27):
        spans = [
            layer_span(shift, cube_edge)
            for shift in (offset // 9 - 1, offset // 3 % 3 - 1, offset % 3 - 1)
        ]
        facing = blocks[:, :, spans[0][0], spans[1][0], spans[2][0]]
        picked = jnp.take(facing, neighbour_ids[:, offset], axis=0)
        padded = padded.at[:, :, spans[0][1], spans[1][1], spans[2][1]].set(picked)
    return padded


def conv_forward(padded, weights, cube_edge):
    result = None
    for offset in range(27):
        start_x, start_y, start_z = (offset // 9, offset // 3 % 3, offset % 3)
        window = padded[
            :,
            :,
            start_x : start_x + cube_edge,
            start_y : start_y + cube_edge,
            start_z : start_z + cube_edge,
        ]
        term = jnp.einsum(
            "oi,bixyz->boxyz", weights[offset], window, preferred_element_type=jnp.float32
        )
        result = term if result is None else result + term
    return result


def conv_transpose(padded, weights, cube_edge):
    result = None
    for offset in range(27):
        start_x, start_y, start_z = (2 - offset // 9, 2 - offset // 3 % 3, 2 - offset % 3)
        window = padded[
            :,
            :,
            start_x : start_x + cube_edge,
            start_y : start_y + cube_edge,
            start_z : start_z + cube_edge,
        ]
        term = jnp.einsum(
            "oi,boxyz->bixyz", weights[offset], window, preferred_element_type=jnp.float32
        )
        result = term if result is None else result + term
    return result


def conv_weights(padded, grads, cube_edge):
    terms = []
    for offset in range(27):
        start_x, start_y, start_z = (offset // 9, offset // 3 % 3, offset % 3)
        window = padded[
            :,
            :,
            start_x : start_x + cube_edge,
            start_y : start_y + cube_edge,
            start_z : start_z + cube_edge,
        ]
        terms.append(
            jnp.einsum("boxyz,bixyz->oi", grads, window, preferred_element_type=jnp.float32)
        )
    return jnp.stack(terms)


def split_fine(values, half_edge):
    rows, channels = (values.shape[0], values.shape[1])
    shaped = values.reshape(rows, channels, half_edge, 2, half_edge, 2, half_edge, 2)
    return shaped.transpose(0, 1, 3, 5, 7, 2, 4, 6).reshape(rows, channels, 8, half_edge**3)


def join_fine(values, half_edge):
    rows, channels = (values.shape[0], values.shape[1])
    shaped = values.reshape(rows, channels, 2, 2, 2, half_edge, half_edge, half_edge)
    return shaped.transpose(0, 1, 5, 2, 6, 3, 7, 4).reshape(rows, channels, 8 * half_edge**3)


def split_block(values, half_edge):
    rows, channels = (values.shape[0], values.shape[1])
    shaped = values.reshape(rows, channels, 2, half_edge, 2, half_edge, 2, half_edge)
    return shaped.transpose(0, 1, 2, 4, 6, 3, 5, 7).reshape(rows, channels, 8, half_edge**3)


def join_block(values, half_edge):
    rows, channels = (values.shape[0], values.shape[1])
    shaped = values.reshape(rows, channels, 2, 2, 2, half_edge, half_edge, half_edge)
    return shaped.transpose(0, 1, 2, 5, 3, 6, 4, 7).reshape(rows, channels, 8 * half_edge**3)


def rim_lookup(own_bricks, exports, forward):
    voxels = own_bricks.shape[2]
    outgoing = jnp.take(own_bricks, exports, axis=0)
    if forward:
        arrived = padded_2(outgoing[None, None], (("gx", 0), ("yz", 1)), 1)
    else:
        arrived = padded_2(outgoing[None, None], (("gx", 0), ("yz", 1)), 1)
    arrived = arrived.reshape(-1, own_bricks.shape[1], voxels)
    blank = jnp.zeros((1, own_bricks.shape[1], voxels), own_bricks.dtype)
    return jnp.concatenate([own_bricks, arrived, blank], axis=0)


def activate_coarse(coarse_pre, cotangent):
    coarse_wide = coarse_pre.astype(jnp.float32)
    grad_coarse = (cotangent.astype(jnp.float32) * silu_slope(coarse_wide)).astype(jnp.bfloat16)
    return grad_coarse


def on_device(
    features, occupancy, neighbours, exports, coarse_map, owners, w_sub, w_down, cotangent
):
    bricks = features.shape[0]
    channels = features.shape[1]
    voxels = features.shape[2]
    half_edge = EDGE // 2
    groups = lax.axis_size("yz")
    live = occupancy.astype(jnp.float32).reshape(bricks, 1, EDGE, EDGE, EDGE)
    masked = features * occupancy.astype(jnp.bfloat16)[:, None, :]
    padded_input = pad_bricks(rim_lookup(masked, exports, True), neighbours, EDGE)
    pre_sub = conv_forward(padded_input, w_sub, EDGE) * live
    hidden = jax.nn.silu(pre_sub).astype(jnp.bfloat16)
    strided = split_fine(hidden.reshape(bricks, channels, voxels), half_edge)
    piece = jnp.einsum("toi,bitu->bou", w_down, strided, preferred_element_type=jnp.float32).astype(
        jnp.bfloat16
    )
    cell_of = coarse_map[:, 0]
    octant_of = coarse_map[:, 1]
    owner_of = jnp.take(owners, cell_of)
    group_ids = jnp.arange(groups, dtype=jnp.int32)
    octant_ids = jnp.arange(8, dtype=jnp.int32)
    select = (
        (owner_of[None, None, :] == group_ids[:, None, None])
        & (octant_of[None, None, :] == octant_ids[None, :, None])
    ).astype(jnp.bfloat16)
    outgoing = join_block(
        jnp.einsum("gob,bcu->gcou", select, piece, preferred_element_type=jnp.float32).astype(
            jnp.bfloat16
        ),
        half_edge,
    )
    coarse_pre = lax.all_to_all(outgoing, "yz", split_axis=0, concat_axis=0, tiled=True)
    grad_coarse = activate_coarse(coarse_pre, cotangent)
    returned = split_block(
        lax.all_to_all(grad_coarse, "yz", split_axis=0, concat_axis=0, tiled=True), half_edge
    )
    grad_piece = jnp.einsum(
        "gob,gcou->bcu", select, returned, preferred_element_type=jnp.float32
    ).astype(jnp.bfloat16)
    coarse = jax.nn.silu(coarse_pre.astype(jnp.float32)).astype(jnp.bfloat16)
    down_local = jnp.einsum(
        "bou,bitu->toi", grad_piece, strided, preferred_element_type=jnp.float32
    )
    grad_hidden = join_fine(
        jnp.einsum("toi,bou->bitu", w_down, grad_piece, preferred_element_type=jnp.float32),
        half_edge,
    )
    grad_hidden = grad_hidden.reshape(bricks, channels, EDGE, EDGE, EDGE)
    grad_pre = (grad_hidden * silu_slope(pre_sub) * live).astype(jnp.bfloat16)
    padded_grad = pad_bricks(
        rim_lookup(grad_pre.reshape(bricks, channels, voxels), exports, False), neighbours, EDGE
    )
    grad_input = conv_transpose(padded_grad, w_sub, EDGE) * live
    grad_features = grad_input.reshape(bricks, channels, voxels).astype(jnp.bfloat16)
    sub_local = conv_weights(padded_input, grad_pre, EDGE)
    grad_sub, grad_down = lax.psum((sub_local, down_local), ("gx", "yz"))
    return (coarse, grad_features, grad_sub, grad_down)


def solution(mesh):
    in_specs = (
        P(("gx", "yz"), None, None),
        P(("gx", "yz"), None),
        P(("gx", "yz"), None),
        P(("gx", "yz")),
        P(("gx", "yz"), None),
        P(("gx", "yz")),
        P(),
        P(),
        P(("gx", "yz"), None, None),
    )
    out_specs = (P(("gx", "yz"), None, None), P(("gx", "yz"), None, None), P(), P())
    return jax.shard_map(
        on_device, mesh=mesh, in_specs=in_specs, out_specs=out_specs, check_vma=False
    )
```

profile of v0, /device:TPU:0, one launch (start us, length us, event | category | flops | bytes accessed | tf_op | source)
XLA Modules:
  0.0 806.1 jit_solution(12787594770374967149)
XLA Ops:
  13.5 6.5 collective-permute-start
  38.3 3.1 pad_maximum_fusion.2
  42.7 4.5 collective-permute-start.2
  47.9 3.3 copy.305
  66.5 6.2 pad_maximum_fusion
  72.7 12.1 %copy.306 = bf16[3,3,8,96,512]{3,2,1,0,4:T(8,128)(2,1)} copy(bf16[3,3,8,96,512]{4,3,2,1,0:T(8,128)(2,1)} %pad_maximum_fusion) | data formatting | bytes 14155776 | tf_op jit(solution)/shard_map/concatenate | solution.py:18
  84.8 8.6 %maximum_maximum_fusion = bf16[85,96,8,8,8]{1,0,4,3,2:T(8,128)(2,1)S(1)} fusion(bf16[72,96,8,8,8]{1,0,4,3,2:T(8,128)(2,1)} %bitcast.1018, bf16[12,96,8,8,8]{1,0,4,3,2:T(8,128)(2,1)S(1)} %bitcast.1024, bf16[85]{0:T(256)(128)(2,1)S(1)} %copy-done.96), kind=kLoop, calls=%fused_computation.57 | loop fusion | flops 25067520 | bytes 16613546 | tf_op jit(solution)/shard_map/concatenate | solution.py:139
  95.0 6.4 copy.325
  113.5 2.7 scatter.180
  144.0 5.1 gather_fusion.15
  170.6 4.2 fusion.66
  184.3 4.5 fusion.281
  191.4 2.7 fusion.289
  194.2 2.8 fusion.293
  202.3 2.7 fusion.305
  205.1 2.8 fusion.309
  207.9 3.1 fusion.313
  211.0 2.8 fusion.317
  216.5 2.8 fusion.325
  221.9 2.8 fusion.333
  227.3 2.8 fusion.341
  232.8 2.7 fusion.349
  235.5 2.7 fusion.353
  238.2 2.8 fusion.357
  243.8 2.7 fusion.365
  246.5 2.7 fusion.369
  249.2 2.8 fusion.373
  257.4 37.2 %multiply_convert_fusion.1 = (bf16[12,96,8,8,8]{1,0,4,3,2:T(8,128)(2,1)S(1)}, f32[12,96,8,8,8]{1,0,4,3,2:T(8,128)}) fusion(f32[12,8,8,8]{0,3,2,1:T(8,128)S(1)} %bitcast.1029, bf16[12,96,10,10,10]{1,0,4,3,2:T(8,128)(2,1)} %constant_dynamic-update-slice_fusion.7, bf16[27,96,96]{2,1,0:T(8,128)(2,1)} %param.141, f32[12,8,8,8,96]{4,0,3,2,1:T(8,128)} %fusion.281, ...), kind=kOutput, calls=%fused_computation.88 | convolution fusion | flops 132120576 | bytes 116736000 | tf_op jit(solution)/shard_map/oi,bixyz->boxyz/dot_general | solution.py:64
  302.5 2.8 copy.349
  305.3 55.4 %all_to_all.10 = bf16[8,192,512]{2,1,0:T(8,128)(2,1)S(1)} all-to-all(bf16[8,192,512]{2,1,0:T(8,128)(2,1)} %copy.349), channel_id=1, replica_groups=mesh['gx'=4,'yz'=8] {'yz'}, dimensions={0} | all-to-all | bytes 3145728 | tf_op jit(solution)/shard_map/all_to_all | solution.py:180
  360.7 3.2 fusion.10
  363.9 4.3 all-to-all-start.1
  368.2 4.2 copy.395
  372.4 16.8 %all-to-all-done.1 = bf16[8,192,512]{2,1,0:T(8,128)(2,1)} async-done(((bf16[8,192,512]{2,1,0:T(8,128)(2,1)}), bf16[8,192,512]{2,1,0:T(8,128)(2,1)}, u32[]{:S(2)}, u32[]{:S(2)}) %all-to-all-start.1) | async-done | bytes 1572896 | tf_op jit(solution)/shard_map/all_to_all | solution.py:183
  389.2 3.2 copy.350
  392.4 3.5 copy.351
  396.0 3.6 reshape.2536
  407.3 2.9 gather_fusion.29
  413.1 5.0 collective-permute-start.4
  418.1 3.0 fusion.72
  456.2 4.5 collective-permute-start.6
  466.5 132.7 %all-reduce.5.cloned.1.call-done = (f32[27,96,96]{2,1,0:T(8,128)}, f32[8,192,96]{1,0,2:T(8,128)}) async-done(((f32[27,96,96]{2,1,0:T(8,128)}, f32[8,192,96]{1,0,2:T(8,128)}), (f32[27,96,96]{2,1,0:T(8,128)}, f32[8,192,96]{1,0,2:T(8,128)})) %all-reduce.5.cloned.1.call-update) | async-done | bytes 1585168 | tf_op jit(solution)/shard_map/psum | solution.py:204
  601.5 6.2 pad_maximum_fusion.1
  607.8 12.1 %copy.460 = bf16[3,3,8,96,512]{3,2,1,0,4:T(8,128)(2,1)} copy(bf16[3,3,8,96,512]{4,3,2,1,0:T(8,128)(2,1)} %pad_maximum_fusion.1) | data formatting | bytes 14155776 | tf_op jit(solution)/shard_map/concatenate | solution.py:139
  619.8 8.6 %maximum_maximum_fusion.1 = bf16[85,96,8,8,8]{1,0,4,3,2:T(8,128)(2,1)S(1)} fusion(bf16[72,96,8,8,8]{1,0,4,3,2:T(8,128)(2,1)} %bitcast.1017, bf16[12,96,8,8,8]{1,0,4,3,2:T(8,128)(2,1)S(1)} %multiply_convert_fusion, bf16[85]{0:T(256)(128)(2,1)S(1)} %copy-done.97), kind=kLoop, calls=%fused_computation.58 | loop fusion | flops 25067520 | bytes 16613546 | tf_op jit(solution)/shard_map/concatenate | solution.py:139
  634.5 6.3 copy.375
  666.3 5.1 gather_fusion.43
  671.5 2.8 copy.381
  676.4 2.8 copy.369
  687.4 3.1 fusion.279
  690.5 2.7 fusion.283
  693.2 2.8 fusion.287
  701.3 2.7 fusion.299
  704.0 2.8 fusion.303
  709.4 3.0 fusion.311
  715.2 2.8 fusion.319
  720.6 2.7 fusion.327
  726.0 2.8 fusion.335
  731.4 2.7 fusion.343
  736.8 2.8 fusion.351
  742.3 2.7 fusion.359
  745.0 2.7 fusion.363
  747.7 2.8 fusion.367
  758.6 35.2 %fusion.1 = bf16[12,96,8,8,8]{1,0,4,3,2:T(8,128)(2,1)S(1)} fusion(f32[12,8,8,8,96]{4,0,3,2,1:T(8,128)} %fusion.279, f32[12,8,8,8,96]{4,0,3,2,1:T(8,128)} %fusion.283, f32[12,8,8,8,96]{4,0,3,2,1:T(8,128)} %fusion.287, f32[12,8,8,8,96]{4,0,3,2,1:T(8,128)} %fusion.291, f32[12,8,8,8,96]{4,0,3,2,1:T(8,128)} %fusion.295, f32[12,8,8,8,96]{4,0,3,2,1:T(8,128)} %fusion.299, ...), kind=kOutput, calls=%fused_computation.66 | convolution fusion | flops 129761280 | bytes 114376704 | tf_op jit(solution)/shard_map/oi,boxyz->bixyz/dot_general | solution.py:82
  (507 shorter events, 280.5 us)
Async XLA Ops:
  7.2 289.4 %copy-start = (bf16[8,192,96]{2,1,0:T(8,128)(2,1)S(1)}, bf16[8,192,96]{2,1,0:T(8,128)(2,1)}, u32[]{:S(2)}) copy-start(bf16[8,192,96]{2,1,0:T(8,128)(2,1)} %param.142) | copy-start | bytes 884740
  7.2 12.8 %copy-start.11 = (s32[12,27]{1,0:T(8,128)S(1)}, s32[12,27]{1,0:T(8,128)}, u32[]{:S(2)}) copy-start(s32[12,27]{1,0:T(8,128)} %param.137) | copy-start | bytes 3892
  7.2 13.6 %copy-start.95 = (s32[12,2]{0,1:T(2,128)S(1)}, s32[12,2]{0,1:T(2,128)}, u32[]{:S(2)}) copy-start(s32[12,2]{0,1:T(2,128)} %param.139) | copy-start | bytes 292
  7.2 15.0 %copy-start.5 = (s32[4]{0:T(128)S(1)}, s32[4]{0:T(128)}, u32[]{:S(2)}) copy-start(s32[4]{0:T(128)} %param.140) | copy-start | bytes 52
  7.9 33.5 %copy-start.98 = (pred[8]{0:T(512)(128)(4,1)}, pred[8]{0:T(512)(128)(4,1)S(1)}, u32[]{:S(2)}) copy-start(pred[8]{0:T(512)(128)(4,1)S(1)} %compare_and_fusion.27) | copy-start | bytes 28
  8.6 32.8 %copy-start.33 = (s32[1024]{0:T(1024)}, s32[1024]{0:T(1024)S(1)}, u32[]{:S(2)}) copy-start(s32[1024]{0:T(1024)S(1)} %pad_clamp_fusion.28) | copy-start | bytes 12292
  11.4 30.0 %copy-start.8 = (bf16[12,96,512]{2,1,0:T(8,128)(2,1)}, bf16[12,96,512]{2,1,0:T(8,128)(2,1)S(1)}, u32[]{:S(2)}) copy-start(bf16[12,96,512]{2,1,0:T(8,128)(2,1)S(1)} %broadcast_multiply_fusion) | copy-start | bytes 3538948
  12.2 26.1 %collective-permute-start.1 = (bf16[1,1,8,96,512]{4,3,2,1,0:T(8,128)(2,1)S(1)}, bf16[1,1,8,96,512]{4,3,2,1,0:T(8,128)(2,1)S(1)}, u32[]{:S(2)}, u32[]{:S(2)}) collective-permute-start(bf16[1,1,8,96,512]{4,3,2,1,0:T(8,128)(2,1)S(1)} %select_bitcast_fusion.1), channel_id=1, source_target_pairs={{8,0},{16,8},{24,16},{9,1},{17,9},{25,17},{10,2},{18,10},{26,18},{... | collective-permute-start | bytes 2359304 | tf_op jit(solution)/shard_map/ppermute | solution.py:17
  13.5 24.8 %collective-permute-start = (bf16[1,1,8,96,512]{4,3,2,1,0:T(8,128)(2,1)S(1)}, bf16[1,1,8,96,512]{4,3,2,1,0:T(8,128)(2,1)}, u32[]{:S(2)}, u32[]{:S(2)}) collective-permute-start(bf16[1,1,8,96,512]{4,3,2,1,0:T(8,128)(2,1)S(1)} %select_bitcast_fusion.1), channel_id=1, source_target_pairs={{0,8},{8,16},{16,24},{1,9},{9,17},{17,25},{2,10},{10,18},{18,26},{... | collective-permute-start | bytes 2359304 | tf_op jit(solution)/shard_map/ppermute | solution.py:16
  20.3 26.9 %copy-start.52 = (s32[12]{0:T(128)}, s32[12]{0:T(128)S(1)}, u32[]{:S(2)}) copy-start(s32[12]{0:T(128)S(1)} %get-tuple-element.700) | copy-start | bytes 148
  20.3 26.9 %copy-start.70 = (s32[12]{0:T(128)}, s32[12]{0:T(128)S(1)}, u32[]{:S(2)}) copy-start(s32[12]{0:T(128)S(1)} %get-tuple-element.699) | copy-start | bytes 148
  20.8 9.8 %copy-start.64 = (s32[12]{0:T(128)}, s32[12]{0:T(128)S(1)}, u32[]{:S(2)}) copy-start(s32[12]{0:T(128)S(1)} %get-tuple-element.686) | copy-start | bytes 148
  20.8 26.3 %copy-start.53 = (s32[12]{0:T(128)}, s32[12]{0:T(128)S(1)}, u32[]{:S(2)}) copy-start(s32[12]{0:T(128)S(1)} %get-tuple-element.698) | copy-start | bytes 148
  20.9 26.3 %copy-start.54 = (s32[12]{0:T(128)}, s32[12]{0:T(128)S(1)}, u32[]{:S(2)}) copy-start(s32[12]{0:T(128)S(1)} %get-tuple-element.696) | copy-start | bytes 148
  20.9 26.3 %copy-start.55 = (s32[12]{0:T(128)}, s32[12]{0:T(128)S(1)}, u32[]{:S(2)}) copy-start(s32[12]{0:T(128)S(1)} %get-tuple-element.697) | copy-start | bytes 148
  20.9 26.3 %copy-start.56 = (s32[12]{0:T(128)}, s32[12]{0:T(128)S(1)}, u32[]{:S(2)}) copy-start(s32[12]{0:T(128)S(1)} %get-tuple-element.694) | copy-start | bytes 148
  20.9 26.3 %copy-start.57 = (s32[12]{0:T(128)}, s32[12]{0:T(128)S(1)}, u32[]{:S(2)}) copy-start(s32[12]{0:T(128)S(1)} %get-tuple-element.695) | copy-start | bytes 148
  20.9 26.3 %copy-start.58 = (s32[12]{0:T(128)}, s32[12]{0:T(128)S(1)}, u32[]{:S(2)}) copy-start(s32[12]{0:T(128)S(1)} %get-tuple-element.692) | copy-start | bytes 148
  20.9 26.3 %copy-start.59 = (s32[12]{0:T(128)}, s32[12]{0:T(128)S(1)}, u32[]{:S(2)}) copy-start(s32[12]{0:T(128)S(1)} %get-tuple-element.693) | copy-start | bytes 148
  20.9 26.3 %copy-start.60 = (s32[12]{0:T(128)}, s32[12]{0:T(128)S(1)}, u32[]{:S(2)}) copy-start(s32[12]{0:T(128)S(1)} %get-tuple-element.690) | copy-start | bytes 148
  20.9 26.3 %copy-start.61 = (s32[12]{0:T(128)}, s32[12]{0:T(128)S(1)}, u32[]{:S(2)}) copy-start(s32[12]{0:T(128)S(1)} %get-tuple-element.691) | copy-start | bytes 148
  20.9 26.3 %copy-start.62 = (s32[12]{0:T(128)}, s32[12]{0:T(128)S(1)}, u32[]{:S(2)}) copy-start(s32[12]{0:T(128)S(1)} %get-tuple-element.688) | copy-start | bytes 148
  20.9 26.3 %copy-start.63 = (s32[12]{0:T(128)}, s32[12]{0:T(128)S(1)}, u32[]{:S(2)}) copy-start(s32[12]{0:T(128)S(1)} %get-tuple-element.689) | copy-start | bytes 148
  21.0 26.3 %copy-start.66 = (s32[12]{0:T(128)}, s32[12]{0:T(128)S(1)}, u32[]{:S(2)}) copy-start(s32[12]{0:T(128)S(1)} %get-tuple-element.684) | copy-start | bytes 148
  21.0 26.3 %copy-start.67 = (s32[12]{0:T(128)}, s32[12]{0:T(128)S(1)}, u32[]{:S(2)}) copy-start(s32[12]{0:T(128)S(1)} %get-tuple-element.685) | copy-start | bytes 148
  21.0 26.3 %copy-start.68 = (s32[12]{0:T(128)}, s32[12]{0:T(128)S(1)}, u32[]{:S(2)}) copy-start(s32[12]{0:T(128)S(1)} %get-tuple-element.682) | copy-start | bytes 148
  21.0 26.3 %copy-start.69 = (s32[12]{0:T(128)}, s32[12]{0:T(128)S(1)}, u32[]{:S(2)}) copy-start(s32[12]{0:T(128)S(1)} %get-tuple-element.683) | copy-start | bytes 148
  21.0 26.3 %copy-start.71 = (s32[12]{0:T(128)}, s32[12]{0:T(128)S(1)}, u32[]{:S(2)}) copy-start(s32[12]{0:T(128)S(1)} %get-tuple-element.681) | copy-start | bytes 148
  25.2 87.7 %copy-start.29 = (s32[1024]{0:T(1024)}, s32[1024]{0:T(1024)S(1)}, u32[]{:S(2)}) copy-start(s32[1024]{0:T(1024)S(1)} %pad_clamp_fusion.27) | copy-start | bytes 12292
  30.0 88.1 %copy-start.30 = (s32[1024]{0:T(1024)}, s32[1024]{0:T(1024)S(1)}, u32[]{:S(2)}) copy-start(s32[1024]{0:T(1024)S(1)} %pad_clamp_fusion.9) | copy-start | bytes 12292
  30.0 87.5 %copy-start.31 = (s32[1024]{0:T(1024)}, s32[1024]{0:T(1024)S(1)}, u32[]{:S(2)}) copy-start(s32[1024]{0:T(1024)S(1)} %pad_clamp_fusion.7) | copy-start | bytes 12292
  30.7 86.2 %copy-start.32 = (s32[1024]{0:T(1024)}, s32[1024]{0:T(1024)S(1)}, u32[]{:S(2)}) copy-start(s32[1024]{0:T(1024)S(1)} %pad_clamp_fusion.3) | copy-start | bytes 12292
  41.4 25.0 %collective-permute-start.3 = (bf16[3,1,8,96,512]{4,3,2,1,0:T(8,128)(2,1)}, bf16[3,1,8,96,512]{4,3,2,1,0:T(8,128)(2,1)}, u32[]{:S(2)}, u32[]{:S(2)}) collective-permute-start(bf16[3,1,8,96,512]{4,3,2,1,0:T(8,128)(2,1)} %pad_maximum_fusion.2), channel_id=1, source_target_pairs={{1,0},{2,1},{3,2},{4,3},{5,4},{6,5},{7,6},{9,8},{10,9},{11,10},{12... | collective-permute-start | bytes 7077896 | tf_op jit(solution)/shard_map/ppermute | solution.py:17
  42.7 23.7 %collective-permute-start.2 = (bf16[3,1,8,96,512]{4,3,2,1,0:T(8,128)(2,1)}, bf16[3,1,8,96,512]{4,3,2,1,0:T(8,128)(2,1)}, u32[]{:S(2)}, u32[]{:S(2)}) collective-permute-start(bf16[3,1,8,96,512]{4,3,2,1,0:T(8,128)(2,1)} %pad_maximum_fusion.2), channel_id=1, source_target_pairs={{0,1},{1,2},{2,3},{3,4},{4,5},{5,6},{6,7},{8,9},{9,10},{10,11},{11... | collective-permute-start | bytes 7077896 | tf_op jit(solution)/shard_map/ppermute | solution.py:16
  52.1 350.5 %copy-start.12 = (f32[12,512]{0,1:T(8,128)}, f32[12,512]{0,1:T(8,128)S(1)}, u32[]{:S(2)}) copy-start(f32[12,512]{0,1:T(8,128)S(1)} %copy.457) | copy-start | bytes 73732
  72.7 12.1 %copy-start.96 = (bf16[85]{0:T(256)(128)(2,1)S(1)}, bf16[85]{0:T(256)(128)(2,1)}, u32[]{:S(2)}) copy-start(bf16[85]{0:T(256)(128)(2,1)} %pad.231.clone) | copy-start | bytes 514
  153.3 21.5 %copy-start.88 = (pred[12]{0:T(512)(128)(4,1)S(1)}, pred[12]{0:T(512)(128)(4,1)}, u32[]{:S(2)}) copy-start(pred[12]{0:T(512)(128)(4,1)} %get-tuple-element.810) | copy-start | bytes 40
  153.3 22.3 %copy-start.14 = (bf16[12,96,8]{1,2,0:T(8,128)(2,1)S(1)}, bf16[12,96,8]{1,2,0:T(8,128)(2,1)}, u32[]{:S(2)}) copy-start(bf16[12,96,8]{1,2,0:T(8,128)(2,1)} %gather_fusion.17) | copy-start | bytes 55300
  153.3 22.3 %copy-start.47 = (pred[12]{0:T(512)(128)(4,1)S(1)}, pred[12]{0:T(512)(128)(4,1)}, u32[]{:S(2)}) copy-start(pred[12]{0:T(512)(128)(4,1)} %get-tuple-element.809) | copy-start | bytes 40
  153.3 23.0 %copy-start.86 = (pred[12]{0:T(512)(128)(4,1)S(1)}, pred[12]{0:T(512)(128)(4,1)}, u32[]{:S(2)}) copy-start(pred[12]{0:T(512)(128)(4,1)} %get-tuple-element.808) | copy-start | bytes 40
  153.3 23.9 %copy-start.44 = (pred[12]{0:T(512)(128)(4,1)S(1)}, pred[12]{0:T(512)(128)(4,1)}, u32[]{:S(2)}) copy-start(pred[12]{0:T(512)(128)(4,1)} %get-tuple-element.807) | copy-start | bytes 40
  153.4 24.5 %copy-start.79 = (pred[12]{0:T(512)(128)(4,1)S(1)}, pred[12]{0:T(512)(128)(4,1)}, u32[]{:S(2)}) copy-start(pred[12]{0:T(512)(128)(4,1)} %get-tuple-element.806) | copy-start | bytes 40
  153.4 25.2 %copy-start.41 = (pred[12]{0:T(512)(128)(4,1)S(1)}, pred[12]{0:T(512)(128)(4,1)}, u32[]{:S(2)}) copy-start(pred[12]{0:T(512)(128)(4,1)} %get-tuple-element.805) | copy-start | bytes 40
  153.4 25.9 %copy-start.77 = (pred[12]{0:T(512)(128)(4,1)S(1)}, pred[12]{0:T(512)(128)(4,1)}, u32[]{:S(2)}) copy-start(pred[12]{0:T(512)(128)(4,1)} %get-tuple-element.804) | copy-start | bytes 40
  153.4 26.5 %copy-start.38 = (pred[12]{0:T(512)(128)(4,1)S(1)}, pred[12]{0:T(512)(128)(4,1)}, u32[]{:S(2)}) copy-start(pred[12]{0:T(512)(128)(4,1)} %get-tuple-element.803) | copy-start | bytes 40
  153.4 27.3 %copy-start.83 = (pred[12]{0:T(512)(128)(4,1)S(1)}, pred[12]{0:T(512)(128)(4,1)}, u32[]{:S(2)}) copy-start(pred[12]{0:T(512)(128)(4,1)} %get-tuple-element.802) | copy-start | bytes 40
  153.4 28.1 %copy-start.36 = (pred[12]{0:T(512)(128)(4,1)S(1)}, pred[12]{0:T(512)(128)(4,1)}, u32[]{:S(2)}) copy-start(pred[12]{0:T(512)(128)(4,1)} %get-tuple-element.801) | copy-start | bytes 40
  153.4 28.8 %copy-start.74 = (pred[12]{0:T(512)(128)(4,1)S(1)}, pred[12]{0:T(512)(128)(4,1)}, u32[]{:S(2)}) copy-start(pred[12]{0:T(512)(128)(4,1)} %get-tuple-element.800) | copy-start | bytes 40
  153.4 29.5 %copy-start.34 = (pred[12]{0:T(512)(128)(4,1)S(1)}, pred[12]{0:T(512)(128)(4,1)}, u32[]{:S(2)}) copy-start(pred[12]{0:T(512)(128)(4,1)} %get-tuple-element.799) | copy-start | bytes 40
  153.4 30.2 %copy-start.72 = (pred[12]{0:T(512)(128)(4,1)S(1)}, pred[12]{0:T(512)(128)(4,1)}, u32[]{:S(2)}) copy-start(pred[12]{0:T(512)(128)(4,1)} %get-tuple-element.798) | copy-start | bytes 40
  153.4 30.8 %copy-start.18 = (bf16[27,96,96]{2,1,0:T(8,128)(2,1)S(1)}, bf16[27,96,96]{2,1,0:T(8,128)(2,1)}, u32[]{:S(2)}) copy-start(bf16[27,96,96]{2,1,0:T(8,128)(2,1)} %param.141) | copy-start | bytes 1492996
  305.3 55.4 %copy-start.23 = (bf16[8,192,512]{2,1,0:T(8,128)(2,1)S(1)}, bf16[8,192,512]{2,1,0:T(8,128)(2,1)}, u32[]{:S(2)}) copy-start(bf16[8,192,512]{2,1,0:T(8,128)(2,1)} %param.143) | copy-start | bytes 4718596
  363.9 25.4 %all-to-all-start.1 = ((bf16[8,192,512]{2,1,0:T(8,128)(2,1)}), bf16[8,192,512]{2,1,0:T(8,128)(2,1)}, u32[]{:S(2)}, u32[]{:S(2)}) async-start(bf16[8,192,512]{2,1,0:T(8,128)(2,1)} %get-tuple-element.762), calls=%async_computation.1 | async-start | bytes 3145728 | tf_op jit(solution)/shard_map/all_to_all | solution.py:183
  368.2 231.0 %all-reduce.5.cloned.1.call-start = ((), (), s32[]{:S(2)}) async-start(), calls=%async_computation.2 | async-start | bytes 4227072 | tf_op jit(solution)/shard_map/psum | solution.py:204
  411.5 9.5 %copy-start.3 = (bf16[12,96,10,10,10]{1,0,4,3,2:T(8,128)(2,1)S(1)}, bf16[12,96,10,10,10]{1,0,4,3,2:T(8,128)(2,1)}, u32[]{:S(2)}) copy-start(bf16[12,96,10,10,10]{1,0,4,3,2:T(8,128)(2,1)} %constant_dynamic-update-slice_fusion.7) | copy-start | bytes 6912004
  411.5 41.6 %collective-permute-start.5 = (bf16[1,1,8,96,512]{4,3,2,1,0:T(8,128)(2,1)S(1)}, bf16[1,1,8,96,512]{4,3,2,1,0:T(8,128)(2,1)S(1)}, u32[]{:S(2)}, u32[]{:S(2)}) collective-permute-start(bf16[1,1,8,96,512]{4,3,2,1,0:T(8,128)(2,1)S(1)} %select_bitcast_fusion), channel_id=1, source_target_pairs={{8,0},{16,8},{24,16},{9,1},{17,9},{25,17},{10,2},{18,10},{26,18},{... | collective-permute-start | bytes 2359304 | tf_op jit(solution)/shard_map/ppermute | solution.py:17
  413.1 40.0 %collective-permute-start.4 = (bf16[1,1,8,96,512]{4,3,2,1,0:T(8,128)(2,1)S(1)}, bf16[1,1,8,96,512]{4,3,2,1,0:T(8,128)(2,1)S(1)}, u32[]{:S(2)}, u32[]{:S(2)}) collective-permute-start(bf16[1,1,8,96,512]{4,3,2,1,0:T(8,128)(2,1)S(1)} %select_bitcast_fusion), channel_id=1, source_target_pairs={{0,8},{8,16},{16,24},{1,9},{9,17},{17,25},{2,10},{10,18},{18,26},{... | collective-permute-start | bytes 2359304 | tf_op jit(solution)/shard_map/ppermute | solution.py:16
  453.0 9.3 %copy-start.16 = (bf16[1,1,8,96,512]{4,3,2,1,0:T(8,128)(2,1)}, bf16[1,1,8,96,512]{4,3,2,1,0:T(8,128)(2,1)S(1)}, u32[]{:S(2)}) copy-start(bf16[1,1,8,96,512]{4,3,2,1,0:T(8,128)(2,1)S(1)} %collective-permute-done.5) | copy-start | bytes 2359300
  453.1 9.3 %copy-start.17 = (bf16[1,1,8,96,512]{4,3,2,1,0:T(8,128)(2,1)}, bf16[1,1,8,96,512]{4,3,2,1,0:T(8,128)(2,1)S(1)}, u32[]{:S(2)}) copy-start(bf16[1,1,8,96,512]{4,3,2,1,0:T(8,128)(2,1)S(1)} %collective-permute-done.4) | copy-start | bytes 2359300
  454.8 146.7 %collective-permute-start.7 = (bf16[3,1,8,96,512]{4,3,2,1,0:T(8,128)(2,1)}, bf16[3,1,8,96,512]{4,3,2,1,0:T(8,128)(2,1)}, u32[]{:S(2)}, u32[]{:S(2)}) collective-permute-start(bf16[3,1,8,96,512]{4,3,2,1,0:T(8,128)(2,1)} %pad_maximum_fusion.3), channel_id=1, source_target_pairs={{1,0},{2,1},{3,2},{4,3},{5,4},{6,5},{7,6},{9,8},{10,9},{11,10},{12... | collective-permute-start | bytes 7077896 | tf_op jit(solution)/shard_map/ppermute | solution.py:17
  456.2 145.3 %collective-permute-start.6 = (bf16[3,1,8,96,512]{4,3,2,1,0:T(8,128)(2,1)}, bf16[3,1,8,96,512]{4,3,2,1,0:T(8,128)(2,1)}, u32[]{:S(2)}, u32[]{:S(2)}) collective-permute-start(bf16[3,1,8,96,512]{4,3,2,1,0:T(8,128)(2,1)} %pad_maximum_fusion.3), channel_id=1, source_target_pairs={{0,1},{1,2},{2,3},{3,4},{4,5},{5,6},{6,7},{8,9},{9,10},{10,11},{11... | collective-permute-start | bytes 7077896 | tf_op jit(solution)/shard_map/ppermute | solution.py:16
  607.8 12.1 %copy-start.97 = (bf16[85]{0:T(256)(128)(2,1)S(1)}, bf16[85]{0:T(256)(128)(2,1)}, u32[]{:S(2)}) copy-start(bf16[85]{0:T(256)(128)(2,1)} %pad.231.clone) | copy-start | bytes 514
  687.4 68.5 %copy-start.4 = (bf16[12,96,10,10,10]{1,0,4,3,2:T(8,128)(2,1)}, bf16[12,96,10,10,10]{1,0,4,3,2:T(8,128)(2,1)S(1)}, u32[]{:S(2)}) copy-start(bf16[12,96,10,10,10]{1,0,4,3,2:T(8,128)(2,1)S(1)} %constant_dynamic-update-slice_fusion) | copy-start | bytes 6912004
  758.6 40.2 %copy-start.1 = (bf16[8,192,96]{2,1,0:T(8,128)(2,1)S(1)}, bf16[8,192,96]{2,1,0:T(8,128)(2,1)}, u32[]{:S(2)}) copy-start(bf16[8,192,96]{2,1,0:T(8,128)(2,1)} %param.142) | copy-start | bytes 884740
  (48 other events, 218.5 us)
Sparse Core Ops, SparseCore 0:
  466.7 132.4 all-reduce.4
where the time goes:
time: 815 us; the launch traced here: 806 us
  matrix products  260 us (32%)
  local copies, waits for them, and re-layouts  183 us (22%)
  waiting for transfers between devices  149 us (18%)
  other arithmetic  112 us (14%)
  blocking collectives  55.4 us (7%)
  starting transfers between devices  30.3 us (4%)
  between operations  16.4 us (2%)
    psum x1, waiting for transfers between devices, on_device(): grad_sub, grad_down = lax.psum((sub_local, down_local), ('gx', 'yz'))  133 us
    dot_general x27, matrix products, conv_forward(): jnp.einsum('oi,bixyz->boxyz', weights[offset], window, preferred_element_...  110 us
    dot_general x27, matrix products, conv_transpose(): jnp.einsum('oi,boxyz->bixyz', weights[offset], window, preferred_element_...  106 us
    gather x54, local copies, waits for them, and re-layouts, pad_bricks(): picked = jnp.take(facing, neighbour_ids[:, offset], axis=0)  63.4 us
    all_to_all x1, blocking collectives, on_device(): lax.all_to_all(outgoing, 'yz', split_axis=0, concat_axis=0, tiled=True)  55.4 us
    dot_general x27, matrix products, conv_weights(): jnp.einsum('boxyz,bixyz->oi', grads, window, preferred_element_type=jnp.f...  39.1 us
    scatter x52, other arithmetic, pad_bricks(): padded = padded.at[:, :, spans[0][1], spans[1][1], spans[2][1]].set(picked)  35.7 us
    another operation x50, local copies, waits for them, and re-layouts, pad_bricks(): picked = jnp.take(facing, neighbour_ids[:, offset], axis=0)  33.3 us
  transfers between devices with their start and end apart: 10, of which 2 were waited for; matrix products, arithmetic and copies ran while one was open for 10% of the time, Pallas kernels for 0%

commit v1 on v0

--- a/solution.py
+++ b/solution.py
@@ -2,6 +2,7 @@
 import jax.numpy as jnp
 from jax import lax
 from jax.sharding import PartitionSpec as P
+from jax.lax import axis_index, axis_size, ppermute
 
 EDGE = 8
 
@@ -148,6 +149,25 @@
 def on_device(
     features, occupancy, neighbours, exports, coarse_map, owners, w_sub, w_down, cotangent
 ):
+
+    def bind_pages(arr_in):
+        y2 = axis_size("yz")
+        y_new, known = (y2, axis_index("yz"))
+        ready = list(arr_in.shape)
+        block_out = arr_in.shape[0] // y_new
+        ready[0] = block_out
+        arr_out = ready[0]
+        ready[0] = arr_out * y_new
+        next_value = jnp.zeros(ready, arr_in.dtype)
+        for p in tuple(range(y_new)):
+            answer = lax.dynamic_slice_in_dim(arr_in, (known ^ p) * block_out, block_out, axis=0)
+            if p:
+                answer = ppermute(answer, "yz", tuple(((u, u ^ p) for u in range(y_new))))
+            next_value = lax.dynamic_update_slice_in_dim(
+                next_value, answer, (known ^ p) * arr_out, axis=0
+            )
+        return next_value
+
     bricks = features.shape[0]
     channels = features.shape[1]
     voxels = features.shape[2]
@@ -177,7 +197,7 @@
         ),
         half_edge,
     )
-    coarse_pre = lax.all_to_all(outgoing, "yz", split_axis=0, concat_axis=0, tiled=True)
+    coarse_pre = bind_pages(outgoing)
     grad_coarse = activate_coarse(coarse_pre, cotangent)
     returned = split_block(
         lax.all_to_all(grad_coarse, "yz", split_axis=0, concat_axis=0, tiled=True), half_edge

time: 815 us -> 843 us (1.034)
  blocking collectives: 55.4 us -> 0 us
  starting transfers between devices: 30.3 us -> 67.5 us
  waiting for transfers between devices: 149 us -> 183 us
  local copies, waits for them, and re-layouts: 183 us -> 194 us
    all_to_all x1 -> x0, blocking collectives: 55.4 us -> none  [on_device(): lax.all_to_all(outgoing, 'yz', split_axis=0, concat_axis=0, tiled=True)]
    ppermute x0 -> x7, starting transfers between devices: none -> 37.2 us  [bind_pages(): answer = ppermute(answer, 'yz', tuple(((u, u ^ p) for u in range(y_new))))]
    ppermute x0 -> x7, waiting for transfers between devices: none -> 33.5 us  [bind_pages(): answer = ppermute(answer, 'yz', tuple(((u, u ^ p) for u in range(y_new))))]
  transfers between devices with their start and end apart: 10 -> 17, of which waited for: 2 -> 5; matrix products, arithmetic and copies ran while one was open for 10% -> 11% of each run, Pallas kernels for 0% -> 0%
where the time goes in v1:
time: 843 us; the launch traced here: 834 us
  matrix products  260 us (31%)
  local copies, waits for them, and re-layouts  194 us (23%)
  waiting for transfers between devices  183 us (22%)
  other arithmetic  113 us (13%)
  starting transfers between devices  67.5 us (8%)
  between operations  16.5 us (2%)
    psum x1, waiting for transfers between devices, on_device(): grad_sub, grad_down = lax.psum((sub_local, down_local), ('gx', 'yz'))  133 us
    dot_general x27, matrix products, conv_forward(): jnp.einsum('oi,bixyz->boxyz', weights[offset], window, preferred_element_...  110 us
    dot_general x27, matrix products, conv_transpose(): jnp.einsum('oi,boxyz->bixyz', weights[offset], window, preferred_element_...  106 us
    gather x54, local copies, waits for them, and re-layouts, pad_bricks(): picked = jnp.take(facing, neighbour_ids[:, offset], axis=0)  63.4 us
    dot_general x27, matrix products, conv_weights(): jnp.einsum('boxyz,bixyz->oi', grads, window, preferred_element_type=jnp.f...  39.1 us
    ppermute x7, starting transfers between devices, bind_pages(): answer = ppermute(answer, 'yz', tuple(((u, u ^ p) for u in range(y_new))))  37.2 us
    scatter x52, other arithmetic, pad_bricks(): padded = padded.at[:, :, spans[0][1], spans[1][1], spans[2][1]].set(picked)  35.6 us
    ppermute x7, waiting for transfers between devices, bind_pages(): answer = ppermute(answer, 'yz', tuple(((u, u ^ p) for u in range(y_new))))  33.5 us
  transfers between devices with their start and end apart: 17, of which 5 were waited for; matrix products, arithmetic and copies ran while one was open for 11% of the time, Pallas kernels for 0%

profile of v1, /device:TPU:0, one launch (start us, length us, event | category | flops | bytes accessed | tf_op | source)
XLA Modules:
  0.0 834.1 jit_solution(11515094739823182406)
XLA Ops:
  13.5 6.5 collective-permute-start
  38.2 3.1 pad_maximum_fusion.2
  42.6 4.5 collective-permute-start.2
  47.8 3.3 copy.312
  66.3 6.2 pad_maximum_fusion
  72.6 12.1 %copy.313 = bf16[3,3,8,96,512]{3,2,1,0,4:T(8,128)(2,1)} copy(bf16[3,3,8,96,512]{4,3,2,1,0:T(8,128)(2,1)} %pad_maximum_fusion) | data formatting | bytes 14155776 | tf_op jit(solution)/shard_map/concatenate | solution.py:19
  84.6 8.6 %maximum_maximum_fusion = bf16[85,96,8,8,8]{1,0,4,3,2:T(8,128)(2,1)S(1)} fusion(bf16[72,96,8,8,8]{1,0,4,3,2:T(8,128)(2,1)} %bitcast.1018, bf16[12,96,8,8,8]{1,0,4,3,2:T(8,128)(2,1)S(1)} %bitcast.1025, bf16[85]{0:T(256)(128)(2,1)S(1)} %copy-done.96), kind=kLoop, calls=%fused_computation.57 | loop fusion | flops 25067520 | bytes 16613546 | tf_op jit(solution)/shard_map/concatenate | solution.py:140
  94.9 6.4 copy.332
  144.0 5.1 gather_fusion.15
  170.5 4.3 fusion.66
  184.2 4.5 fusion.281
  188.7 2.7 fusion.285
  194.1 2.8 fusion.293
  199.6 2.7 fusion.301
  202.3 2.7 fusion.305
  205.1 2.8 fusion.309
  207.9 3.1 fusion.313
  216.3 2.8 fusion.325
  221.8 2.7 fusion.333
  227.1 2.8 fusion.341
  232.6 2.7 fusion.349
  235.4 2.7 fusion.353
  238.1 2.8 fusion.357
  243.6 2.7 fusion.365
  246.4 2.7 fusion.369
  249.1 2.8 fusion.373
  257.3 37.1 %multiply_convert_fusion.1 = (bf16[12,96,8,8,8]{1,0,4,3,2:T(8,128)(2,1)S(1)}, f32[12,96,8,8,8]{1,0,4,3,2:T(8,128)}) fusion(f32[12,8,8,8]{0,3,2,1:T(8,128)S(1)} %bitcast.1029, bf16[12,96,10,10,10]{1,0,4,3,2:T(8,128)(2,1)} %constant_dynamic-update-slice_fusion.15, bf16[27,96,96]{2,1,0:T(8,128)(2,1)} %param.141, f32[12,8,8,8,96]{4,0,3,2,1:T(8,128)} %fusion.281, ...), kind=kOutput, calls=%fused_computation.88 | convolution fusion | flops 132120576 | bytes 116736000 | tf_op jit(solution)/shard_map/oi,bixyz->boxyz/dot_general | solution.py:65
  302.3 5.4 constant_dynamic-slice_fusion
  307.7 33.0 %collective-permute-start.9 = (bf16[1,192,512]{1,0,2:T(2,128)(2,1)}, bf16[1,192,512]{1,0,2:T(2,128)(2,1)}, u32[]{:S(2)}, u32[]{:S(2)}) collective-permute-start(bf16[1,192,512]{1,0,2:T(2,128)(2,1)} %get-tuple-element.763), channel_id=1, source_target_pairs={{0,6},{1,7},{2,4},{3,5},{4,2},{5,3},{6,0},{7,1},{8,14},{9,15},{10,... | collective-permute-start | bytes 589832 | tf_op jit(solution)/shard_map/ppermute | solution.py:165
  344.9 9.0 %collective-permute-done.9 = bf16[1,192,512]{1,0,2:T(2,128)(2,1)} collective-permute-done((bf16[1,192,512]{1,0,2:T(2,128)(2,1)}, bf16[1,192,512]{1,0,2:T(2,128)(2,1)}, u32[]{:S(2)}, u32[]{:S(2)}) %collective-permute-start.9) | collective-permute-done | bytes 196640 | tf_op jit(solution)/shard_map/ppermute | solution.py:165
  355.1 10.1 %collective-permute-done.7 = bf16[1,192,512]{1,0,2:T(2,128)(2,1)} collective-permute-done((bf16[1,192,512]{1,0,2:T(2,128)(2,1)}, bf16[1,192,512]{1,0,2:T(2,128)(2,1)}, u32[]{:S(2)}, u32[]{:S(2)}) %collective-permute-start.7) | collective-permute-done | bytes 196640 | tf_op jit(solution)/shard_map/ppermute | solution.py:165
  369.5 14.4 %collective-permute-done.6 = bf16[1,192,512]{1,0,2:T(2,128)(2,1)} collective-permute-done((bf16[1,192,512]{1,0,2:T(2,128)(2,1)}, bf16[1,192,512]{1,0,2:T(2,128)(2,1)}, u32[]{:S(2)}, u32[]{:S(2)}) %collective-permute-start.6) | collective-permute-done | bytes 196640 | tf_op jit(solution)/shard_map/ppermute | solution.py:165
  386.8 4.6 fusion.10
  391.5 4.3 all-to-all-start
  395.8 4.4 copy.409
  400.3 16.9 %all-to-all-done = bf16[8,192,512]{2,1,0:T(8,128)(2,1)} async-done(((bf16[8,192,512]{2,1,0:T(8,128)(2,1)}), bf16[8,192,512]{2,1,0:T(8,128)(2,1)}, u32[]{:S(2)}, u32[]{:S(2)}) %all-to-all-start) | async-done | bytes 1572896 | tf_op jit(solution)/shard_map/all_to_all | solution.py:203
  417.1 3.2 copy.364
  420.4 3.5 copy.365
  423.8 3.6 reshape.2536
  435.5 2.9 gather_fusion.29
  441.2 5.0 collective-permute-start.11
  446.2 3.0 fusion.72
  484.4 4.5 collective-permute-start.13
  494.7 132.6 %all-reduce.5.cloned.1.call-done = (f32[27,96,96]{2,1,0:T(8,128)}, f32[8,192,96]{1,0,2:T(8,128)}) async-done(((f32[27,96,96]{2,1,0:T(8,128)}, f32[8,192,96]{1,0,2:T(8,128)}), (f32[27,96,96]{2,1,0:T(8,128)}, f32[8,192,96]{1,0,2:T(8,128)})) %all-reduce.5.cloned.1.call-update) | async-done | bytes 1585168 | tf_op jit(solution)/shard_map/psum | solution.py:224
  629.6 6.2 pad_maximum_fusion.1
  635.9 12.1 %copy.474 = bf16[3,3,8,96,512]{3,2,1,0,4:T(8,128)(2,1)} copy(bf16[3,3,8,96,512]{4,3,2,1,0:T(8,128)(2,1)} %pad_maximum_fusion.1) | data formatting | bytes 14155776 | tf_op jit(solution)/shard_map/concatenate | solution.py:140
  647.9 8.6 %maximum_maximum_fusion.1 = bf16[85,96,8,8,8]{1,0,4,3,2:T(8,128)(2,1)S(1)} fusion(bf16[72,96,8,8,8]{1,0,4,3,2:T(8,128)(2,1)} %bitcast.1017, bf16[12,96,8,8,8]{1,0,4,3,2:T(8,128)(2,1)S(1)} %multiply_convert_fusion, bf16[85]{0:T(256)(128)(2,1)S(1)} %copy-done.97), kind=kLoop, calls=%fused_computation.58 | loop fusion | flops 25067520 | bytes 16613546 | tf_op jit(solution)/shard_map/concatenate | solution.py:140
  662.6 6.3 copy.389
  694.4 5.1 gather_fusion.43
  699.6 2.8 copy.395
  704.4 2.8 copy.383
  715.5 3.1 fusion.279
  721.3 2.8 fusion.287
  726.7 2.7 fusion.295
  732.2 2.8 fusion.303
  737.6 3.0 fusion.311
  743.2 2.8 fusion.319
  754.0 2.8 fusion.335
  759.4 2.7 fusion.343
  764.9 2.8 fusion.351
  770.4 2.7 fusion.359
  775.8 2.8 fusion.367
  781.3 2.7 fusion.375
  786.7 35.1 %fusion.1 = bf16[12,96,8,8,8]{1,0,4,3,2:T(8,128)(2,1)S(1)} fusion(f32[12,8,8,8,96]{4,0,3,2,1:T(8,128)} %fusion.279, f32[12,8,8,8,96]{4,0,3,2,1:T(8,128)} %fusion.283, f32[12,8,8,8,96]{4,0,3,2,1:T(8,128)} %fusion.287, f32[12,8,8,8,96]{4,0,3,2,1:T(8,128)} %fusion.291, f32[12,8,8,8,96]{4,0,3,2,1:T(8,128)} %fusion.295, f32[12,8,8,8,96]{4,0,3,2,1:T(8,128)} %fusion.299, ...), kind=kOutput, calls=%fused_computation.66 | convolution fusion | flops 129761280 | bytes 114376704 | tf_op jit(solution)/shard_map/oi,boxyz->bixyz/dot_general | solution.py:83
  (537 shorter events, 301.0 us)
Async XLA Ops:
  7.2 289.3 %copy-start = (bf16[8,192,96]{2,1,0:T(8,128)(2,1)S(1)}, bf16[8,192,96]{2,1,0:T(8,128)(2,1)}, u32[]{:S(2)}) copy-start(bf16[8,192,96]{2,1,0:T(8,128)(2,1)} %param.142) | copy-start | bytes 884740
  7.2 12.8 %copy-start.11 = (s32[12,27]{1,0:T(8,128)S(1)}, s32[12,27]{1,0:T(8,128)}, u32[]{:S(2)}) copy-start(s32[12,27]{1,0:T(8,128)} %param.137) | copy-start | bytes 3892
  7.2 13.6 %copy-start.95 = (s32[12,2]{0,1:T(2,128)S(1)}, s32[12,2]{0,1:T(2,128)}, u32[]{:S(2)}) copy-start(s32[12,2]{0,1:T(2,128)} %param.139) | copy-start | bytes 292
  7.2 14.9 %copy-start.5 = (s32[4]{0:T(128)S(1)}, s32[4]{0:T(128)}, u32[]{:S(2)}) copy-start(s32[4]{0:T(128)} %param.140) | copy-start | bytes 52
  7.9 33.4 %copy-start.98 = (pred[8]{0:T(512)(128)(4,1)}, pred[8]{0:T(512)(128)(4,1)S(1)}, u32[]{:S(2)}) copy-start(pred[8]{0:T(512)(128)(4,1)S(1)} %compare_and_fusion.27) | copy-start | bytes 28
  8.6 32.7 %copy-start.33 = (s32[1024]{0:T(1024)}, s32[1024]{0:T(1024)S(1)}, u32[]{:S(2)}) copy-start(s32[1024]{0:T(1024)S(1)} %pad_clamp_fusion.28) | copy-start | bytes 12292
  11.4 29.9 %copy-start.8 = (bf16[12,96,512]{2,1,0:T(8,128)(2,1)}, bf16[12,96,512]{2,1,0:T(8,128)(2,1)S(1)}, u32[]{:S(2)}) copy-start(bf16[12,96,512]{2,1,0:T(8,128)(2,1)S(1)} %broadcast_multiply_fusion) | copy-start | bytes 3538948
  12.2 26.0 %collective-permute-start.1 = (bf16[1,1,8,96,512]{4,3,2,1,0:T(8,128)(2,1)S(1)}, bf16[1,1,8,96,512]{4,3,2,1,0:T(8,128)(2,1)S(1)}, u32[]{:S(2)}, u32[]{:S(2)}) collective-permute-start(bf16[1,1,8,96,512]{4,3,2,1,0:T(8,128)(2,1)S(1)} %select_bitcast_fusion.1), channel_id=1, source_target_pairs={{8,0},{16,8},{24,16},{9,1},{17,9},{25,17},{10,2},{18,10},{26,18},{... | collective-permute-start | bytes 2359304 | tf_op jit(solution)/shard_map/ppermute | solution.py:18
  13.5 24.7 %collective-permute-start = (bf16[1,1,8,96,512]{4,3,2,1,0:T(8,128)(2,1)S(1)}, bf16[1,1,8,96,512]{4,3,2,1,0:T(8,128)(2,1)}, u32[]{:S(2)}, u32[]{:S(2)}) collective-permute-start(bf16[1,1,8,96,512]{4,3,2,1,0:T(8,128)(2,1)S(1)} %select_bitcast_fusion.1), channel_id=1, source_target_pairs={{0,8},{8,16},{16,24},{1,9},{9,17},{17,25},{2,10},{10,18},{18,26},{... | collective-permute-start | bytes 2359304 | tf_op jit(solution)/shard_map/ppermute | solution.py:17
  20.3 27.4 %copy-start.52 = (s32[12]{0:T(128)}, s32[12]{0:T(128)S(1)}, u32[]{:S(2)}) copy-start(s32[12]{0:T(128)S(1)} %get-tuple-element.700) | copy-start | bytes 148
  20.3 27.4 %copy-start.70 = (s32[12]{0:T(128)}, s32[12]{0:T(128)S(1)}, u32[]{:S(2)}) copy-start(s32[12]{0:T(128)S(1)} %get-tuple-element.699) | copy-start | bytes 148
  20.9 26.8 %copy-start.53 = (s32[12]{0:T(128)}, s32[12]{0:T(128)S(1)}, u32[]{:S(2)}) copy-start(s32[12]{0:T(128)S(1)} %get-tuple-element.698) | copy-start | bytes 148
  20.9 26.8 %copy-start.54 = (s32[12]{0:T(128)}, s32[12]{0:T(128)S(1)}, u32[]{:S(2)}) copy-start(s32[12]{0:T(128)S(1)} %get-tuple-element.696) | copy-start | bytes 148
  20.9 26.8 %copy-start.55 = (s32[12]{0:T(128)}, s32[12]{0:T(128)S(1)}, u32[]{:S(2)}) copy-start(s32[12]{0:T(128)S(1)} %get-tuple-element.697) | copy-start | bytes 148
  20.9 26.8 %copy-start.56 = (s32[12]{0:T(128)}, s32[12]{0:T(128)S(1)}, u32[]{:S(2)}) copy-start(s32[12]{0:T(128)S(1)} %get-tuple-element.694) | copy-start | bytes 148
  20.9 26.8 %copy-start.57 = (s32[12]{0:T(128)}, s32[12]{0:T(128)S(1)}, u32[]{:S(2)}) copy-start(s32[12]{0:T(128)S(1)} %get-tuple-element.695) | copy-start | bytes 148
  20.9 26.8 %copy-start.58 = (s32[12]{0:T(128)}, s32[12]{0:T(128)S(1)}, u32[]{:S(2)}) copy-start(s32[12]{0:T(128)S(1)} %get-tuple-element.692) | copy-start | bytes 148
  20.9 26.8 %copy-start.59 = (s32[12]{0:T(128)}, s32[12]{0:T(128)S(1)}, u32[]{:S(2)}) copy-start(s32[12]{0:T(128)S(1)} %get-tuple-element.693) | copy-start | bytes 148
  20.9 26.8 %copy-start.60 = (s32[12]{0:T(128)}, s32[12]{0:T(128)S(1)}, u32[]{:S(2)}) copy-start(s32[12]{0:T(128)S(1)} %get-tuple-element.690) | copy-start | bytes 148
  20.9 26.8 %copy-start.61 = (s32[12]{0:T(128)}, s32[12]{0:T(128)S(1)}, u32[]{:S(2)}) copy-start(s32[12]{0:T(128)S(1)} %get-tuple-element.691) | copy-start | bytes 148
  21.0 26.8 %copy-start.62 = (s32[12]{0:T(128)}, s32[12]{0:T(128)S(1)}, u32[]{:S(2)}) copy-start(s32[12]{0:T(128)S(1)} %get-tuple-element.688) | copy-start | bytes 148
  21.0 26.8 %copy-start.63 = (s32[12]{0:T(128)}, s32[12]{0:T(128)S(1)}, u32[]{:S(2)}) copy-start(s32[12]{0:T(128)S(1)} %get-tuple-element.689) | copy-start | bytes 148
  21.0 26.8 %copy-start.66 = (s32[12]{0:T(128)}, s32[12]{0:T(128)S(1)}, u32[]{:S(2)}) copy-start(s32[12]{0:T(128)S(1)} %get-tuple-element.684) | copy-start | bytes 148
  21.0 26.8 %copy-start.67 = (s32[12]{0:T(128)}, s32[12]{0:T(128)S(1)}, u32[]{:S(2)}) copy-start(s32[12]{0:T(128)S(1)} %get-tuple-element.685) | copy-start | bytes 148
  21.0 26.8 %copy-start.68 = (s32[12]{0:T(128)}, s32[12]{0:T(128)S(1)}, u32[]{:S(2)}) copy-start(s32[12]{0:T(128)S(1)} %get-tuple-element.682) | copy-start | bytes 148
  21.0 26.8 %copy-start.69 = (s32[12]{0:T(128)}, s32[12]{0:T(128)S(1)}, u32[]{:S(2)}) copy-start(s32[12]{0:T(128)S(1)} %get-tuple-element.683) | copy-start | bytes 148
  21.0 26.8 %copy-start.71 = (s32[12]{0:T(128)}, s32[12]{0:T(128)S(1)}, u32[]{:S(2)}) copy-start(s32[12]{0:T(128)S(1)} %get-tuple-element.681) | copy-start | bytes 148
  25.1 87.7 %copy-start.29 = (s32[1024]{0:T(1024)}, s32[1024]{0:T(1024)S(1)}, u32[]{:S(2)}) copy-start(s32[1024]{0:T(1024)S(1)} %pad_clamp_fusion.27) | copy-start | bytes 12292
  29.9 88.1 %copy-start.30 = (s32[1024]{0:T(1024)}, s32[1024]{0:T(1024)S(1)}, u32[]{:S(2)}) copy-start(s32[1024]{0:T(1024)S(1)} %pad_clamp_fusion.9) | copy-start | bytes 12292
  30.0 87.5 %copy-start.31 = (s32[1024]{0:T(1024)}, s32[1024]{0:T(1024)S(1)}, u32[]{:S(2)}) copy-start(s32[1024]{0:T(1024)S(1)} %pad_clamp_fusion.7) | copy-start | bytes 12292
  30.6 86.2 %copy-start.32 = (s32[1024]{0:T(1024)}, s32[1024]{0:T(1024)S(1)}, u32[]{:S(2)}) copy-start(s32[1024]{0:T(1024)S(1)} %pad_clamp_fusion.3) | copy-start | bytes 12292
  41.3 25.0 %collective-permute-start.3 = (bf16[3,1,8,96,512]{4,3,2,1,0:T(8,128)(2,1)}, bf16[3,1,8,96,512]{4,3,2,1,0:T(8,128)(2,1)}, u32[]{:S(2)}, u32[]{:S(2)}) collective-permute-start(bf16[3,1,8,96,512]{4,3,2,1,0:T(8,128)(2,1)} %pad_maximum_fusion.2), channel_id=1, source_target_pairs={{1,0},{2,1},{3,2},{4,3},{5,4},{6,5},{7,6},{9,8},{10,9},{11,10},{12... | collective-permute-start | bytes 7077896 | tf_op jit(solution)/shard_map/ppermute | solution.py:18
  42.6 23.7 %collective-permute-start.2 = (bf16[3,1,8,96,512]{4,3,2,1,0:T(8,128)(2,1)}, bf16[3,1,8,96,512]{4,3,2,1,0:T(8,128)(2,1)}, u32[]{:S(2)}, u32[]{:S(2)}) collective-permute-start(bf16[3,1,8,96,512]{4,3,2,1,0:T(8,128)(2,1)} %pad_maximum_fusion.2), channel_id=1, source_target_pairs={{0,1},{1,2},{2,3},{3,4},{4,5},{5,6},{6,7},{8,9},{9,10},{10,11},{11... | collective-permute-start | bytes 7077896 | tf_op jit(solution)/shard_map/ppermute | solution.py:17
  52.0 205.3 %copy-start.12 = (f32[12,512]{0,1:T(8,128)}, f32[12,512]{0,1:T(8,128)S(1)}, u32[]{:S(2)}) copy-start(f32[12,512]{0,1:T(8,128)S(1)} %copy.471) | copy-start | bytes 73732
  153.3 21.5 %copy-start.88 = (pred[12]{0:T(512)(128)(4,1)S(1)}, pred[12]{0:T(512)(128)(4,1)}, u32[]{:S(2)}) copy-start(pred[12]{0:T(512)(128)(4,1)} %get-tuple-element.818) | copy-start | bytes 40
  153.3 22.4 %copy-start.15 = (bf16[12,96,8]{1,2,0:T(8,128)(2,1)S(1)}, bf16[12,96,8]{1,2,0:T(8,128)(2,1)}, u32[]{:S(2)}) copy-start(bf16[12,96,8]{1,2,0:T(8,128)(2,1)} %gather_fusion.17) | copy-start | bytes 55300
  153.3 22.4 %copy-start.47 = (pred[12]{0:T(512)(128)(4,1)S(1)}, pred[12]{0:T(512)(128)(4,1)}, u32[]{:S(2)}) copy-start(pred[12]{0:T(512)(128)(4,1)} %get-tuple-element.817) | copy-start | bytes 40
  153.3 23.0 %copy-start.86 = (pred[12]{0:T(512)(128)(4,1)S(1)}, pred[12]{0:T(512)(128)(4,1)}, u32[]{:S(2)}) copy-start(pred[12]{0:T(512)(128)(4,1)} %get-tuple-element.816) | copy-start | bytes 40
  153.3 23.9 %copy-start.45 = (pred[12]{0:T(512)(128)(4,1)S(1)}, pred[12]{0:T(512)(128)(4,1)}, u32[]{:S(2)}) copy-start(pred[12]{0:T(512)(128)(4,1)} %get-tuple-element.815) | copy-start | bytes 40
  153.3 24.6 %copy-start.80 = (pred[12]{0:T(512)(128)(4,1)S(1)}, pred[12]{0:T(512)(128)(4,1)}, u32[]{:S(2)}) copy-start(pred[12]{0:T(512)(128)(4,1)} %get-tuple-element.814) | copy-start | bytes 40
  153.3 25.2 %copy-start.43 = (pred[12]{0:T(512)(128)(4,1)S(1)}, pred[12]{0:T(512)(128)(4,1)}, u32[]{:S(2)}) copy-start(pred[12]{0:T(512)(128)(4,1)} %get-tuple-element.813) | copy-start | bytes 40
  153.4 25.9 %copy-start.78 = (pred[12]{0:T(512)(128)(4,1)S(1)}, pred[12]{0:T(512)(128)(4,1)}, u32[]{:S(2)}) copy-start(pred[12]{0:T(512)(128)(4,1)} %get-tuple-element.812) | copy-start | bytes 40
  153.4 26.5 %copy-start.41 = (pred[12]{0:T(512)(128)(4,1)S(1)}, pred[12]{0:T(512)(128)(4,1)}, u32[]{:S(2)}) copy-start(pred[12]{0:T(512)(128)(4,1)} %get-tuple-element.811) | copy-start | bytes 40
  153.4 27.2 %copy-start.84 = (pred[12]{0:T(512)(128)(4,1)S(1)}, pred[12]{0:T(512)(128)(4,1)}, u32[]{:S(2)}) copy-start(pred[12]{0:T(512)(128)(4,1)} %get-tuple-element.810) | copy-start | bytes 40
  153.4 28.1 %copy-start.39 = (pred[12]{0:T(512)(128)(4,1)S(1)}, pred[12]{0:T(512)(128)(4,1)}, u32[]{:S(2)}) copy-start(pred[12]{0:T(512)(128)(4,1)} %get-tuple-element.809) | copy-start | bytes 40
  153.4 28.8 %copy-start.76 = (pred[12]{0:T(512)(128)(4,1)S(1)}, pred[12]{0:T(512)(128)(4,1)}, u32[]{:S(2)}) copy-start(pred[12]{0:T(512)(128)(4,1)} %get-tuple-element.808) | copy-start | bytes 40
  153.4 29.4 %copy-start.37 = (pred[12]{0:T(512)(128)(4,1)S(1)}, pred[12]{0:T(512)(128)(4,1)}, u32[]{:S(2)}) copy-start(pred[12]{0:T(512)(128)(4,1)} %get-tuple-element.807) | copy-start | bytes 40
  153.4 30.1 %copy-start.74 = (pred[12]{0:T(512)(128)(4,1)S(1)}, pred[12]{0:T(512)(128)(4,1)}, u32[]{:S(2)}) copy-start(pred[12]{0:T(512)(128)(4,1)} %get-tuple-element.806) | copy-start | bytes 40
  153.4 30.7 %copy-start.19 = (bf16[27,96,96]{2,1,0:T(8,128)(2,1)S(1)}, bf16[27,96,96]{2,1,0:T(8,128)(2,1)}, u32[]{:S(2)}) copy-start(bf16[27,96,96]{2,1,0:T(8,128)(2,1)} %param.141) | copy-start | bytes 1492996
  307.7 46.2 %collective-permute-start.9 = (bf16[1,192,512]{1,0,2:T(2,128)(2,1)}, bf16[1,192,512]{1,0,2:T(2,128)(2,1)}, u32[]{:S(2)}, u32[]{:S(2)}) collective-permute-start(bf16[1,192,512]{1,0,2:T(2,128)(2,1)} %get-tuple-element.763), channel_id=1, source_target_pairs={{0,6},{1,7},{2,4},{3,5},{4,2},{5,3},{6,0},{7,1},{8,14},{9,15},{10,... | collective-permute-start | bytes 589832 | tf_op jit(solution)/shard_map/ppermute | solution.py:165
  340.7 24.5 %collective-permute-start.7 = (bf16[1,192,512]{1,0,2:T(2,128)(2,1)}, bf16[1,192,512]{1,0,2:T(2,128)(2,1)}, u32[]{:S(2)}, u32[]{:S(2)}) collective-permute-start(bf16[1,192,512]{1,0,2:T(2,128)(2,1)} %get-tuple-element.765), channel_id=1, source_target_pairs={{0,4},{1,5},{2,6},{3,7},{4,0},{5,1},{6,2},{7,3},{8,12},{9,13},{10,... | collective-permute-start | bytes 589832 | tf_op jit(solution)/shard_map/ppermute | solution.py:165
  340.7 26.2 %collective-permute-start.5 = (bf16[1,192,512]{1,0,2:T(2,128)(2,1)}, bf16[1,192,512]{1,0,2:T(2,128)(2,1)}, u32[]{:S(2)}, u32[]{:S(2)}) collective-permute-start(bf16[1,192,512]{1,0,2:T(2,128)(2,1)} %get-tuple-element.767), channel_id=1, source_target_pairs={{0,2},{1,3},{2,0},{3,1},{4,6},{5,7},{6,4},{7,5},{8,10},{9,11},{10,... | collective-permute-start | bytes 589832 | tf_op jit(solution)/shard_map/ppermute | solution.py:165
  341.9 26.3 %collective-permute-start.4 = (bf16[1,192,512]{1,0,2:T(2,128)(2,1)}, bf16[1,192,512]{1,0,2:T(2,128)(2,1)}, u32[]{:S(2)}, u32[]{:S(2)}) collective-permute-start(bf16[1,192,512]{1,0,2:T(2,128)(2,1)} %get-tuple-element.768), channel_id=1, source_target_pairs={{0,1},{1,0},{2,3},{3,2},{4,5},{5,4},{6,7},{7,6},{8,9},{9,8},{10,11... | collective-permute-start | bytes 589832 | tf_op jit(solution)/shard_map/ppermute | solution.py:165
  342.2 44.2 %collective-permute-start.10 = (bf16[1,192,512]{1,0,2:T(2,128)(2,1)}, bf16[1,192,512]{1,0,2:T(2,128)(2,1)S(1)}, u32[]{:S(2)}, u32[]{:S(2)}) collective-permute-start(bf16[1,192,512]{1,0,2:T(2,128)(2,1)} %get-tuple-element.762), channel_id=1, source_target_pairs={{0,7},{1,6},{2,5},{3,4},{4,3},{5,2},{6,1},{7,0},{8,15},{9,14},{10,... | collective-permute-start | bytes 589832 | tf_op jit(solution)/shard_map/ppermute | solution.py:165
  353.9 31.2 %collective-permute-start.8 = (bf16[1,192,512]{1,0,2:T(2,128)(2,1)}, bf16[1,192,512]{1,0,2:T(2,128)(2,1)}, u32[]{:S(2)}, u32[]{:S(2)}) collective-permute-start(bf16[1,192,512]{1,0,2:T(2,128)(2,1)} %get-tuple-element.764), channel_id=1, source_target_pairs={{0,5},{1,4},{2,7},{3,6},{4,1},{5,0},{6,3},{7,2},{8,13},{9,12},{10,... | collective-permute-start | bytes 589832 | tf_op jit(solution)/shard_map/ppermute | solution.py:165
  365.2 18.6 %collective-permute-start.6 = (bf16[1,192,512]{1,0,2:T(2,128)(2,1)}, bf16[1,192,512]{1,0,2:T(2,128)(2,1)}, u32[]{:S(2)}, u32[]{:S(2)}) collective-permute-start(bf16[1,192,512]{1,0,2:T(2,128)(2,1)} %get-tuple-element.766), channel_id=1, source_target_pairs={{0,3},{1,2},{2,1},{3,0},{4,7},{5,6},{6,5},{7,4},{8,11},{9,10},{10,... | collective-permute-start | bytes 589832 | tf_op jit(solution)/shard_map/ppermute | solution.py:165
  391.5 25.7 %all-to-all-start = ((bf16[8,192,512]{2,1,0:T(8,128)(2,1)}), bf16[8,192,512]{2,1,0:T(8,128)(2,1)}, u32[]{:S(2)}, u32[]{:S(2)}) async-start(bf16[8,192,512]{2,1,0:T(8,128)(2,1)} %get-tuple-element.770), calls=%async_computation | async-start | bytes 3145728 | tf_op jit(solution)/shard_map/all_to_all | solution.py:203
  395.8 231.5 %all-reduce.5.cloned.1.call-start = ((), (), s32[]{:S(2)}) async-start(), calls=%async_computation.1 | async-start | bytes 4227072 | tf_op jit(solution)/shard_map/psum | solution.py:224
  439.6 41.6 %collective-permute-start.12 = (bf16[1,1,8,96,512]{4,3,2,1,0:T(8,128)(2,1)S(1)}, bf16[1,1,8,96,512]{4,3,2,1,0:T(8,128)(2,1)S(1)}, u32[]{:S(2)}, u32[]{:S(2)}) collective-permute-start(bf16[1,1,8,96,512]{4,3,2,1,0:T(8,128)(2,1)S(1)} %select_bitcast_fusion), channel_id=1, source_target_pairs={{8,0},{16,8},{24,16},{9,1},{17,9},{25,17},{10,2},{18,10},{26,18},{... | collective-permute-start | bytes 2359304 | tf_op jit(solution)/shard_map/ppermute | solution.py:18
  441.2 40.0 %collective-permute-start.11 = (bf16[1,1,8,96,512]{4,3,2,1,0:T(8,128)(2,1)S(1)}, bf16[1,1,8,96,512]{4,3,2,1,0:T(8,128)(2,1)S(1)}, u32[]{:S(2)}, u32[]{:S(2)}) collective-permute-start(bf16[1,1,8,96,512]{4,3,2,1,0:T(8,128)(2,1)S(1)} %select_bitcast_fusion), channel_id=1, source_target_pairs={{0,8},{8,16},{16,24},{1,9},{9,17},{17,25},{2,10},{10,18},{18,26},{... | collective-permute-start | bytes 2359304 | tf_op jit(solution)/shard_map/ppermute | solution.py:17
  482.9 146.7 %collective-permute-start.14 = (bf16[3,1,8,96,512]{4,3,2,1,0:T(8,128)(2,1)}, bf16[3,1,8,96,512]{4,3,2,1,0:T(8,128)(2,1)}, u32[]{:S(2)}, u32[]{:S(2)}) collective-permute-start(bf16[3,1,8,96,512]{4,3,2,1,0:T(8,128)(2,1)} %pad_maximum_fusion.3), channel_id=1, source_target_pairs={{1,0},{2,1},{3,2},{4,3},{5,4},{6,5},{7,6},{9,8},{10,9},{11,10},{12... | collective-permute-start | bytes 7077896 | tf_op jit(solution)/shard_map/ppermute | solution.py:18
  484.4 145.3 %collective-permute-start.13 = (bf16[3,1,8,96,512]{4,3,2,1,0:T(8,128)(2,1)}, bf16[3,1,8,96,512]{4,3,2,1,0:T(8,128)(2,1)}, u32[]{:S(2)}, u32[]{:S(2)}) collective-permute-start(bf16[3,1,8,96,512]{4,3,2,1,0:T(8,128)(2,1)} %pad_maximum_fusion.3), channel_id=1, source_target_pairs={{0,1},{1,2},{2,3},{3,4},{4,5},{5,6},{6,7},{8,9},{9,10},{10,11},{11... | collective-permute-start | bytes 7077896 | tf_op jit(solution)/shard_map/ppermute | solution.py:17
  715.5 68.6 %copy-start.4 = (bf16[12,96,10,10,10]{1,0,4,3,2:T(8,128)(2,1)}, bf16[12,96,10,10,10]{1,0,4,3,2:T(8,128)(2,1)S(1)}, u32[]{:S(2)}) copy-start(bf16[12,96,10,10,10]{1,0,4,3,2:T(8,128)(2,1)S(1)} %constant_dynamic-update-slice_fusion) | copy-start | bytes 6912004
  786.7 40.2 %copy-start.1 = (bf16[8,192,96]{2,1,0:T(8,128)(2,1)S(1)}, bf16[8,192,96]{2,1,0:T(8,128)(2,1)}, u32[]{:S(2)}) copy-start(bf16[8,192,96]{2,1,0:T(8,128)(2,1)} %param.142) | copy-start | bytes 884740
  (55 other events, 283.1 us)
Sparse Core Ops, SparseCore 0:
  494.8 132.4 all-reduce.4
